TPU v7x, 32 devices: a whole 2x2x4 slice. The times are simulated.
32 devices in a mesh: dp: 8 (over y, x, core), section: 4 (over z).
Axes of the slice: x: 2, y: 2, z: 4, core: 2. Of those that a mesh axis runs over, the one named last changes fastest.
Arguments:
- block_input: bfloat16 [16, 1536, 512], P('dp'), may hold values from -6 to 6
- known_genes: int32 [16, 1536], P('dp'), may hold values 0 or 1
- attn_proj: bfloat16 [2, 512, 1536], replicated, may hold values from -0.25 to 0.25
- attn_out: bfloat16 [2, 512, 512], replicated, may hold values from -2 to 2
- query_bias: float32 [2, 512], replicated, may hold values from -1.5 to 1.5
- value_bias: float32 [2, 512], replicated, may hold values from -0.15 to 0.15
- out_bias: float32 [2, 512], replicated, may hold values from -1.5 to 1.5
- ff_in: bfloat16 [2, 512, 512], replicated, may hold values from -0.25 to 0.25
- ff_out: bfloat16 [2, 512, 512], replicated, may hold values from -0.25 to 0.25
- ff_bias_in: float32 [2, 512], replicated, may hold values from -1.5 to 1.5
- ff_bias_out: float32 [2, 512], replicated, may hold values from -1.5 to 1.5
- norm_gain: float32 [2, 2, 512], replicated, may hold values from 0.1 to 1.9
- norm_shift: float32 [2, 2, 512], replicated, may hold values from -1.5 to 1.5
- cotangent: bfloat16 [16, 1536, 512], P('dp'), may hold values from -6 to 6
Outputs:
- section_outputs: bfloat16 [4, 16, 1536, 512], P('section', 'dp')
- section_input_grads: bfloat16 [4, 16, 1536, 512], P('section', 'dp')
- grad_attn_proj: float32 [2, 512, 1536], P(None, ('dp', 'section'))
- grad_attn_out: float32 [2, 512, 512], P(None, ('dp', 'section'))
- grad_query_bias: float32 [2, 512], P(None, ('dp', 'section'))
- grad_value_bias: float32 [2, 512], P(None, ('dp', 'section'))
- grad_out_bias: float32 [2, 512], P(None, ('dp', 'section'))
- grad_ff_in: float32 [2, 512, 512], P(None, ('dp', 'section'))
- grad_ff_out: float32 [2, 512, 512], P(None, ('dp', 'section'))
- grad_ff_bias_in: float32 [2, 512], P(None, ('dp', 'section'))
- grad_ff_bias_out: float32 [2, 512], P(None, ('dp', 'section'))
- grad_norm_gain: float32 [2, 2, 512], P(None, None, ('dp', 'section'))
- grad_norm_shift: float32 [2, 2, 512], P(None, None, ('dp', 'section'))
All inputs are finite; a program needn't handle non-finite values. No bound on the sum of `known_genes` on one device may be relied on, other than what follows from the above.
Results may differ from a plain program's by a relative error of at most 0.02.
Values may be sent and summed in bfloat16 or wider, within the bound.
No kernel may reach another device: no remote copies, remote signals or barrier semaphores. Data moves between devices by JAX's collectives and lax.ppermute only.
A program may use at most 256 MiB of HBM per device.

v0:
```python
from functools import partial

import jax
import jax.numpy as jnp
from jax import lax
from jax.sharding import PartitionSpec as P

HEADS = 8
HEAD_DIM = 64
LONG = 1024
SHORT = 512


eps_norm = 1e-05
masked_fill = -1e30


def for_sending(x):
    return jax.tree.map(lambda a: a.astype(jnp.bfloat16) if a.dtype == jnp.float32 else a, x)


def shifted(block, axis, distance):
    devices = range(lax.axis_size(axis))
    route = [(i - distance, i) for i in devices if i - distance in devices]
    return lax.ppermute(block, axis, route)


def norm_stats(residual):
    center = residual - jnp.mean(residual, axis=-1, keepdims=True)
    inv_std = lax.rsqrt(jnp.mean(center * center, axis=-1, keepdims=True) + eps_norm)
    return (center * inv_std, inv_std)


def norm_back(grad_out, normed, inv_std, gain_row):
    grad_gain = jnp.sum(grad_out * normed, axis=0)
    grad_shift = jnp.sum(grad_out, axis=0)
    grad_norm = grad_out * gain_row
    grad_resid = inv_std * (
        grad_norm
        - jnp.mean(grad_norm, axis=-1, keepdims=True)
        - normed * jnp.mean(grad_norm * normed, axis=-1, keepdims=True)
    )
    return (grad_resid, grad_gain, grad_shift)


def split_heads(matrix):
    return matrix.reshape(matrix.shape[0], HEADS, HEAD_DIM)


def block_probs(query_block, block_start, key_heads, known_cell):
    block_len = query_block.shape[0]
    length = key_heads.shape[0]
    scores = jnp.einsum(
        "qhd,khd->hqk", query_block, key_heads, preferred_element_type=jnp.float32
    ) * HEAD_DIM ** (-0.5)
    row_ids = block_start + lax.iota(jnp.int32, block_len)
    col_ids = lax.iota(jnp.int32, length)
    allowed = (known_cell[None, :] == 1) | (row_ids[:, None] == col_ids[None, :])
    masked = jnp.where(allowed[None], scores, masked_fill)
    exp_scores = jnp.exp(masked - jnp.max(masked, axis=-1, keepdims=True))
    return exp_scores / jnp.sum(exp_scores, axis=-1, keepdims=True)


def cell_blocks(query_cell):
    length = query_cell.shape[0]
    block_len = min(512, length)
    block_count = length // block_len
    blocks = split_heads(query_cell).reshape(block_count, block_len, HEADS, HEAD_DIM)
    starts = lax.iota(jnp.int32, block_count) * block_len
    return (blocks, starts)


def cell_forward(query_cell, key_cell, value_cell, known_cell):
    length = query_cell.shape[0]
    key_heads = split_heads(key_cell)
    value_heads = split_heads(value_cell)
    query_blocks, starts = cell_blocks(query_cell)

    def one_block(block_pair):
        query_block, block_start = block_pair
        block_prob = block_probs(query_block, block_start, key_heads, known_cell).astype(
            jnp.bfloat16
        )
        mixed_block = jnp.einsum(
            "hqk,khd->qhd", block_prob, value_heads, preferred_element_type=jnp.float32
        )
        return mixed_block.astype(jnp.bfloat16)

    outputs = lax.map(one_block, (query_blocks, starts))
    return outputs.reshape(length, HEADS * HEAD_DIM)


def cell_backward(query_cell, key_cell, value_cell, known_cell, grad_cell):
    length = query_cell.shape[0]
    key_heads = split_heads(key_cell)
    value_heads = split_heads(value_cell)
    query_blocks, starts = cell_blocks(query_cell)
    grad_blocks, unused_starts = cell_blocks(grad_cell)
    scale_attn = HEAD_DIM ** (-0.5)

    def one_block(carry, block_data):
        grad_keys, grad_values = carry
        query_block, grad_block, block_start = block_data
        block_prob = block_probs(query_block, block_start, key_heads, known_cell)
        grad_values = grad_values + jnp.einsum(
            "hqk,qhd->khd",
            block_prob.astype(jnp.bfloat16),
            grad_block,
            preferred_element_type=jnp.float32,
        )
        grad_prob = jnp.einsum(
            "qhd,khd->hqk", grad_block, value_heads, preferred_element_type=jnp.float32
        )
        delta_row = jnp.sum(grad_prob * block_prob, axis=-1, keepdims=True)
        grad_score = (block_prob * (grad_prob - delta_row)).astype(jnp.bfloat16)
        grad_query = (
            jnp.einsum("hqk,khd->qhd", grad_score, key_heads, preferred_element_type=jnp.float32)
            * scale_attn
        )
        grad_keys = (
            grad_keys
            + jnp.einsum(
                "hqk,qhd->khd", grad_score, query_block, preferred_element_type=jnp.float32
            )
            * scale_attn
        )
        return ((grad_keys, grad_values), grad_query)

    zero_heads = jnp.zeros((length, HEADS, HEAD_DIM), jnp.float32)
    (grad_keys, grad_values), grad_queries = lax.scan(
        one_block, (zero_heads, zero_heads), (query_blocks, grad_blocks, starts)
    )
    width = HEADS * HEAD_DIM
    return (
        grad_queries.reshape(length, width),
        grad_keys.reshape(length, width),
        grad_values.reshape(length, width),
    )


def cell_ranges():
    return ((0, LONG), (LONG, SHORT))


def attention_forward(section_in, known_row, weights):
    w_qkv, w_mix, bias_query, bias_value, bias_mix, gain_row, shift_row = weights
    width = w_mix.shape[0]
    projected = jnp.dot(section_in, w_qkv, preferred_element_type=jnp.float32)
    query_all = (projected[:, :width] + bias_query).astype(jnp.bfloat16)
    key_all = projected[:, width : 2 * width].astype(jnp.bfloat16)
    value_all = (projected[:, 2 * width :] + bias_value).astype(jnp.bfloat16)
    pieces = []
    for cell_start, cell_len in cell_ranges():
        pieces.append(
            cell_forward(
                query_all[cell_start : cell_start + cell_len],
                key_all[cell_start : cell_start + cell_len],
                value_all[cell_start : cell_start + cell_len],
                known_row[cell_start : cell_start + cell_len],
            )
        )
    attn_mix = jnp.concatenate(pieces, axis=0)
    residual = (
        section_in.astype(jnp.float32)
        + jnp.dot(attn_mix, w_mix, preferred_element_type=jnp.float32)
        + bias_mix
    )
    normed, inv_std = norm_stats(residual)
    section_out = (normed * gain_row + shift_row).astype(jnp.bfloat16)
    return (section_out, (query_all, key_all, value_all, attn_mix, normed, inv_std))


def attention_backward(section_in, known_row, weights, grad_out):
    w_qkv, w_mix, bias_query, bias_value, bias_mix, gain_row, shift_row = weights
    recomputed, saved = attention_forward(section_in, known_row, weights)
    query_all, key_all, value_all, attn_mix, normed, inv_std = saved
    grad_resid, grad_gain, grad_shift = norm_back(grad_out, normed, inv_std, gain_row)
    grad_branch = grad_resid.astype(jnp.bfloat16)
    grad_w_mix = jnp.dot(attn_mix.T, grad_branch, preferred_element_type=jnp.float32)
    grad_mix = jnp.dot(grad_branch, w_mix.T, preferred_element_type=jnp.float32).astype(
        jnp.bfloat16
    )
    query_parts, key_parts, value_parts = ([], [], [])
    for cell_start, cell_len in cell_ranges():
        cell_end = cell_start + cell_len
        grad_query, grad_key, grad_value = cell_backward(
            query_all[cell_start:cell_end],
            key_all[cell_start:cell_end],
            value_all[cell_start:cell_end],
            known_row[cell_start:cell_end],
            grad_mix[cell_start:cell_end],
        )
        query_parts.append(grad_query)
        key_parts.append(grad_key)
        value_parts.append(grad_value)
    grad_query = jnp.concatenate(query_parts, axis=0)
    grad_value = jnp.concatenate(value_parts, axis=0)
    grad_proj = jnp.concatenate(
        [grad_query, jnp.concatenate(key_parts, axis=0), grad_value], axis=1
    ).astype(jnp.bfloat16)
    grad_w_qkv = jnp.dot(section_in.T, grad_proj, preferred_element_type=jnp.float32)
    grad_in = grad_resid + jnp.dot(grad_proj, w_qkv.T, preferred_element_type=jnp.float32)
    return (
        grad_in.astype(jnp.bfloat16),
        (
            grad_w_qkv,
            grad_w_mix,
            jnp.sum(grad_query, axis=0),
            jnp.sum(grad_value, axis=0),
            jnp.sum(grad_resid, axis=0),
            grad_gain,
            grad_shift,
        ),
    )


def feed_forward(section_in, weights):
    w_up, w_down, bias_up, bias_down, gain_row, shift_row = weights
    pre_act = jnp.dot(section_in, w_up, preferred_element_type=jnp.float32) + bias_up
    hidden = jax.nn.gelu(pre_act, approximate=False).astype(jnp.bfloat16)
    residual = (
        section_in.astype(jnp.float32)
        + jnp.dot(hidden, w_down, preferred_element_type=jnp.float32)
        + bias_down
    )
    normed, inv_std = norm_stats(residual)
    section_out = (normed * gain_row + shift_row).astype(jnp.bfloat16)
    return (section_out, (pre_act, hidden, normed, inv_std))


def feed_backward(section_in, weights, grad_out):
    w_up, w_down, bias_up, bias_down, gain_row, shift_row = weights
    recomputed, saved = feed_forward(section_in, weights)
    pre_act, hidden, normed, inv_std = saved
    grad_resid, grad_gain, grad_shift = norm_back(grad_out, normed, inv_std, gain_row)
    grad_branch = grad_resid.astype(jnp.bfloat16)
    grad_down = jnp.dot(hidden.T, grad_branch, preferred_element_type=jnp.float32)
    grad_hidden = jnp.dot(grad_branch, w_down.T, preferred_element_type=jnp.float32)
    unused_value, gelu_pull = jax.vjp(partial(jax.nn.gelu, approximate=False), pre_act)
    grad_pre = gelu_pull(grad_hidden)[0]
    grad_pre_low = grad_pre.astype(jnp.bfloat16)
    grad_up = jnp.dot(section_in.T, grad_pre_low, preferred_element_type=jnp.float32)
    grad_in = grad_resid + jnp.dot(grad_pre_low, w_up.T, preferred_element_type=jnp.float32)
    return (
        grad_in.astype(jnp.bfloat16),
        (
            grad_up,
            grad_down,
            jnp.sum(grad_pre, axis=0),
            jnp.sum(grad_resid, axis=0),
            grad_gain,
            grad_shift,
        ),
    )


def put_row(row_table, row_value, slot_num, is_valid):
    previous = lax.dynamic_index_in_dim(row_table, slot_num, 0, keepdims=False)
    return lax.dynamic_update_index_in_dim(
        row_table, jnp.where(is_valid, row_value, previous), slot_num, 0
    )


def per_device(
    block_input,
    known_genes,
    attn_proj,
    attn_out,
    query_bias,
    value_bias,
    out_bias,
    ff_in,
    ff_out,
    ff_bias_in,
    ff_bias_out,
    norm_gain,
    norm_shift,
    cotangent,
):
    params = (
        attn_proj,
        attn_out,
        query_bias,
        value_bias,
        out_bias,
        ff_in,
        ff_out,
        ff_bias_in,
        ff_bias_out,
        norm_gain,
        norm_shift,
    )
    section_count = lax.axis_size("section")
    section_num = lax.axis_index("section")
    micro_count = block_input.shape[0]

    def attn_weights(layer_num):
        return (
            attn_proj[layer_num],
            attn_out[layer_num],
            query_bias[layer_num],
            value_bias[layer_num],
            out_bias[layer_num],
            norm_gain[layer_num, 0],
            norm_shift[layer_num, 0],
        )

    def feed_weights(layer_num):
        return (
            ff_in[layer_num],
            ff_out[layer_num],
            ff_bias_in[layer_num],
            ff_bias_out[layer_num],
            norm_gain[layer_num, 1],
            norm_shift[layer_num, 1],
        )

    def zero_grads():
        return tuple((jnp.zeros(tensor.shape, jnp.float32) for tensor in params))

    def spread(layer_num, kind_num, local_grads):
        full_grads = list(zero_grads())
        slot_list = (0, 1, 2, 3, 4) if kind_num == 0 else (5, 6, 7, 8)
        for position, grad_part in zip(slot_list, local_grads[:-2]):
            full_grads[position] = full_grads[position].at[layer_num].set(grad_part)
        full_grads[9] = full_grads[9].at[layer_num, kind_num].set(local_grads[-2])
        full_grads[10] = full_grads[10].at[layer_num, kind_num].set(local_grads[-1])
        return tuple(full_grads)

    def make_forward(branch_num):
        layer_num = branch_num // 2
        if branch_num % 2 == 0:

            def run_section(section_in, known_row):
                return attention_forward(section_in, known_row, attn_weights(layer_num))[0]

        else:

            def run_section(section_in, known_row):
                return feed_forward(section_in, feed_weights(layer_num))[0]

        return run_section

    def make_backward(branch_num):
        layer_num = branch_num // 2
        kind_num = branch_num % 2
        if kind_num == 0:

            def run_back(section_in, known_row, grad_out):
                grad_in, local_grads = attention_backward(
                    section_in, known_row, attn_weights(layer_num), grad_out
                )
                return (grad_in, spread(layer_num, 0, local_grads))

        else:

            def run_back(section_in, known_row, grad_out):
                grad_in, local_grads = feed_backward(section_in, feed_weights(layer_num), grad_out)
                return (grad_in, spread(layer_num, 1, local_grads))

        return run_back

    def skip_forward(section_in, known_row):
        return jnp.zeros_like(section_in)

    def skip_backward(section_in, known_row, grad_out):
        return (jnp.zeros_like(section_in), zero_grads())

    forward_list = [make_forward(branch_num) for branch_num in range(section_count)] + [
        skip_forward
    ]
    backward_list = [make_backward(branch_num) for branch_num in range(section_count)] + [
        skip_backward
    ]
    tick_count = micro_count + section_count - 1

    def forward_tick(tick_num, carry):
        stored, outputs, arrived = carry
        micro_num = tick_num - section_num
        is_valid = (micro_num >= 0) & (micro_num < micro_count)
        slot_num = jnp.clip(micro_num, 0, micro_count - 1)
        fresh_row = lax.dynamic_index_in_dim(block_input, slot_num, 0, keepdims=False)
        section_in = jnp.where(section_num == 0, fresh_row, arrived)
        known_row = lax.dynamic_index_in_dim(known_genes, slot_num, 0, keepdims=False)
        section_out = lax.switch(
            jnp.where(is_valid, section_num, section_count), forward_list, section_in, known_row
        )
        stored = put_row(stored, section_in, slot_num, is_valid)
        outputs = put_row(outputs, section_out, slot_num, is_valid)
        arrived = jax.tree.map(
            lambda part, own: part.astype(own.dtype),
            shifted(for_sending(section_out), "section", 1),
            section_out,
        )
        return (stored, outputs, arrived)

    empty_rows = jnp.zeros_like(block_input)
    stored, outputs, arrived = lax.fori_loop(
        0, tick_count, forward_tick, (empty_rows, empty_rows, empty_rows[0])
    )

    def backward_tick(tick_num, carry):
        totals, in_grads, arrived_back = carry
        micro_num = tick_num - (section_count - 1 - section_num)
        is_valid = (micro_num >= 0) & (micro_num < micro_count)
        slot_num = jnp.clip(micro_num, 0, micro_count - 1)
        cot_row = lax.dynamic_index_in_dim(cotangent, slot_num, 0, keepdims=False)
        grad_seed = jnp.where(section_num == section_count - 1, cot_row, arrived_back).astype(
            jnp.float32
        )
        section_in = lax.dynamic_index_in_dim(stored, slot_num, 0, keepdims=False)
        known_row = lax.dynamic_index_in_dim(known_genes, slot_num, 0, keepdims=False)
        grad_in, section_grads = lax.switch(
            jnp.where(is_valid, section_num, section_count),
            backward_list,
            section_in,
            known_row,
            grad_seed,
        )
        totals = jax.tree.map(jnp.add, totals, section_grads)
        in_grads = put_row(in_grads, grad_in, slot_num, is_valid)
        arrived_back = jax.tree.map(
            lambda part, own: part.astype(own.dtype),
            shifted(for_sending(grad_in), "section", -1),
            grad_in,
        )
        return (totals, in_grads, arrived_back)

    totals, in_grads, arrived_back = lax.fori_loop(
        0, tick_count, backward_tick, (zero_grads(), empty_rows, empty_rows[0])
    )
    (
        total_proj,
        total_mix,
        total_query,
        total_value,
        total_outb,
        total_up,
        total_down,
        total_upb,
        total_downb,
        total_gain,
        total_shift,
    ) = totals
    summed = (
        lax.psum_scatter(total_proj, ("dp", "section"), scatter_dimension=1, tiled=True),
        lax.psum_scatter(total_mix, ("dp", "section"), scatter_dimension=1, tiled=True),
        lax.psum_scatter(total_query, ("dp", "section"), scatter_dimension=1, tiled=True),
        lax.psum_scatter(total_value, ("dp", "section"), scatter_dimension=1, tiled=True),
        lax.psum_scatter(total_outb, ("dp", "section"), scatter_dimension=1, tiled=True),
        lax.psum_scatter(total_up, ("dp", "section"), scatter_dimension=1, tiled=True),
        lax.psum_scatter(total_down, ("dp", "section"), scatter_dimension=1, tiled=True),
        lax.psum_scatter(total_upb, ("dp", "section"), scatter_dimension=1, tiled=True),
        lax.psum_scatter(total_downb, ("dp", "section"), scatter_dimension=1, tiled=True),
        lax.psum_scatter(total_gain, ("dp", "section"), scatter_dimension=2, tiled=True),
        lax.psum_scatter(total_shift, ("dp", "section"), scatter_dimension=2, tiled=True),
    )
    return (
        outputs[None],
        in_grads[None],
        summed[0],
        summed[1],
        summed[2],
        summed[3],
        summed[4],
        summed[5],
        summed[6],
        summed[7],
        summed[8],
        summed[9],
        summed[10],
    )


def solution(mesh):
    placed = (
        P("dp", None, None),
        P("dp", None),
        P(),
        P(),
        P(),
        P(),
        P(),
        P(),
        P(),
        P(),
        P(),
        P(),
        P(),
        P("dp", None, None),
    )
    return jax.shard_map(
        per_device,
        mesh=mesh,
        in_specs=placed,
        out_specs=(
            P("section", "dp", None, None),
            P("section", "dp", None, None),
            P(None, ("dp", "section"), None),
            P(None, ("dp", "section"), None),
            P(None, ("dp", "section")),
            P(None, ("dp", "section")),
            P(None, ("dp", "section")),
            P(None, ("dp", "section"), None),
            P(None, ("dp", "section"), None),
            P(None, ("dp", "section")),
            P(None, ("dp", "section")),
            P(None, None, ("dp", "section")),
            P(None, None, ("dp", "section")),
        ),
        check_vma=False,
    )
```

profile of v0, /device:TPU:0, one launch (start us, length us, event | category | flops | bytes accessed | tf_op | source)
XLA Modules:
  0.0 3618.9 jit_solution(11858217160691885042)
XLA Ops:
  12.3 653.9 %while.203 = (s32[]{:T(128)}, bf16[2,1536,512]{1,2,0:T(8,128)(2,1)}, bf16[2,1536,512]{2,1,0:T(8,128)(2,1)}, bf16[1536,512]{0,1:T(8,128)(2,1)}, s32[]{:T(128)}, /...) while((s32[]{:T(128)}, bf16[2,1536,512]{1,2,0:T(8,128)(2,1)}, ...), condition=%wide.region_26.27_spmd, body=%wide.region_0.26_spmd.sunk | while | flops 4900525056 | bytes 222563936 | solution.py:398
  20.5 128.7 %conditional.5 = (bf16[1536,512]{0,1:T(8,128)(2,1)}) conditional(s32[]{:T(128)} %clamp.19, (bf16[1536,512]{0,1:T(8,128)(2,1)}, bf16[2,512,1536]{2,1,0:T(8,128)(2,1)}, f32[2,512]{1,0:T(2,128)S(1)}, s32[2,1536]{1,0:T(2,128)S(1)}, s32[]{:T(128)}, /*index=5*/f32[2,512]{1,0:T(2,128)S(1)}, bf16[2,512,512]{2,1,0:T(8,128)(2,1)}, ...), branch_computations={%region_1.9_spmd, %region_10.12_spmd, %region_13.21_spmd, %region_... | conditional | flops 4898165760 | bytes 169002368 | solution.py:385
  193.0 128.9 %conditional.5 = (bf16[1536,512]{0,1:T(8,128)(2,1)}) conditional(s32[]{:T(128)} %clamp.19, (bf16[1536,512]{0,1:T(8,128)(2,1)}, bf16[2,512,1536]{2,1,0:T(8,128)(2,1)}, f32[2,512]{1,0:T(2,128)S(1)}, s32[2,1536]{1,0:T(2,128)S(1)}, s32[]{:T(128)}, /*index=5*/f32[2,512]{1,0:T(2,128)S(1)}, bf16[2,512,512]{2,1,0:T(8,128)(2,1)}, ...), branch_computations={%region_1.9_spmd, %region_10.12_spmd, %region_13.21_spmd, %region_... | conditional | flops 4898165760 | bytes 169002368 | solution.py:385
  218.0 81.9 %while.197 = (s32[]{:T(128)}, bf16[2,512,8,64]{1,3,2,0:T(8,128)(2,1)}, s32[1024]{0:T(1024)S(1)}, s32[2]{0:T(128)S(1)}, bf16[2,512,8,64]{1,3,2,0:T(8,128)(2,1)S(1...) while((s32[]{:T(128)}, bf16[2,512,8,64]{1,3,2,0:T(8,128)(2,1)}, ...), condition=%wide.region_5.4_spmd, body=%wide.region_2.3_spmd.sunk | while | flops 1108609536 | bytes 71346296 | solution.py:89
  527.4 106.8 %collective-permute-start.1 = (bf16[1536,512]{0,1:T(8,128)(2,1)}, bf16[1536,512]{0,1:T(8,128)(2,1)}, u32[]{:S(2)}, u32[]{:S(2)}) collective-permute-start(bf16[1536,512]{0,1:T(8,128)(2,1)} %get-tuple-element.3944), channel_id=1, source_target_pairs={{0,1},{1,2},{2,3},{4,5},{5,6},{6,7},{8,9},{9,10},{10,11},{12,13},{... | collective-permute-start | bytes 4718600 | tf_op jit(solution)/shard_map/while/body/eval_jaxpr/ppermute | solution.py:25
  669.4 1485.8 %while.204 = (s32[]{:T(128)}, f32[2,512,1536]{2,1,0:T(8,128)}, f32[2,512,512]{2,1,0:T(8,128)}, f32[2,512]{1,0:T(2,128)}, f32[2,512]{1,0:T(2,128)}, /*index=5*/f3...) while((s32[]{:T(128)}, f32[2,512,1536]{2,1,0:T(8,128)}, ...), condition=%wide.region_95.96_spmd.clone, body=%wide.region_27.95_spmd.clone.sunk | while | flops 15270690816 | bytes 907249152 | solution.py:429
  914.0 398.2 %collective-permute-done = bf16[1536,512]{0,1:T(8,128)(2,1)} collective-permute-done((bf16[1536,512]{0,1:T(8,128)(2,1)}, bf16[1536,512]{0,1:T(8,128)(2,1)}, u32[]{:S(2)}, u32[]{:S(2)}) %collective-permute-start) | collective-permute-done | bytes 1572896 | tf_op jit(solution)/shard_map/while/body/eval_jaxpr/ppermute | solution.py:25
  1321.2 377.9 %conditional.6 = (bf16[1536,512]{0,1:T(8,128)(2,1)}, f32[2,512,1536]{2,1,0:T(8,128)}, f32[2,512,512]{2,1,0:T(8,128)S(1)}, f32[2,512]{1,0:T(2,128)S(1)}, f32[2,51...) conditional(s32[]{:T(128)} %clamp.20, ...), branch_computations={%region_28.51_spmd, %region_52.60_spmd, %region_61.84_spmd, %regio... | conditional | flops 15262021632 | bytes 720589184 | solution.py:413
  1345.3 82.0 %while.199 = (s32[]{:T(128)}, bf16[2,512,8,64]{1,3,2,0:T(8,128)(2,1)}, s32[1024]{0:T(1024)S(1)}, s32[2]{0:T(128)S(1)}, bf16[2,512,8,64]{1,3,2,0:T(8,128)(2,1)S(1...) while((s32[]{:T(128)}, bf16[2,512,8,64]{1,3,2,0:T(8,128)(2,1)}, ...), condition=%wide.region_32.31_spmd, body=%wide.region_29.30_spmd.sunk | while | flops 1108609536 | bytes 71346296 | solution.py:89
  1448.9 153.6 %while.200 = (s32[]{:T(128)}, f32[1024,8,64]{0,2,1:T(8,128)S(1)}, f32[1024,8,64]{0,2,1:T(8,128)}, f32[2,512,8,64]{1,3,2,0:T(8,128)}, bf16[2,512,8,64]{1,3,2,0:T(...) while((s32[]{:T(128)}, f32[1024,8,64]{0,2,1:T(8,128)S(1)}, ...), condition=%wide.region_43.42_spmd.clone, body=%wide.region_39.41_spmd.clone.sunk | while | flops 2751199744 | bytes 238135696 | solution.py:130
  1741.8 377.9 %conditional.6 = (bf16[1536,512]{0,1:T(8,128)(2,1)}, f32[2,512,1536]{2,1,0:T(8,128)}, f32[2,512,512]{2,1,0:T(8,128)S(1)}, f32[2,512]{1,0:T(2,128)S(1)}, f32[2,51...) conditional(s32[]{:T(128)} %clamp.20, ...), branch_computations={%region_28.51_spmd, %region_52.60_spmd, %region_61.84_spmd, %regio... | conditional | flops 15262021632 | bytes 720589184 | solution.py:413
  1765.9 82.1 %while.199 = (s32[]{:T(128)}, bf16[2,512,8,64]{1,3,2,0:T(8,128)(2,1)}, s32[1024]{0:T(1024)S(1)}, s32[2]{0:T(128)S(1)}, bf16[2,512,8,64]{1,3,2,0:T(8,128)(2,1)S(1...) while((s32[]{:T(128)}, bf16[2,512,8,64]{1,3,2,0:T(8,128)(2,1)}, ...), condition=%wide.region_32.31_spmd, body=%wide.region_29.30_spmd.sunk | while | flops 1108609536 | bytes 71346296 | solution.py:89
  1869.5 153.6 %while.200 = (s32[]{:T(128)}, f32[1024,8,64]{0,2,1:T(8,128)S(1)}, f32[1024,8,64]{0,2,1:T(8,128)}, f32[2,512,8,64]{1,3,2,0:T(8,128)}, bf16[2,512,8,64]{1,3,2,0:T(...) while((s32[]{:T(128)}, f32[1024,8,64]{0,2,1:T(8,128)S(1)}, ...), condition=%wide.region_43.42_spmd.clone, body=%wide.region_39.41_spmd.clone.sunk | while | flops 2751199744 | bytes 238135696 | solution.py:130
  2170.7 115.7 %reduce-scatter.34.cloned.1.call-done = f32[16,2]{1,0:T(8,128)} async-done(((f32[512,2]{1,0:T(8,128)}), f32[16,2]{1,0:T(8,128)}) %reduce-scatter.34.cloned.1.call-update) | async-done | bytes 144
  2287.7 130.7 %reduce-scatter.36.cloned.1.call-done = f32[16,2]{1,0:T(8,128)} async-done(((f32[512,2]{1,0:T(8,128)}), f32[16,2]{1,0:T(8,128)}) %reduce-scatter.36.cloned.1.call-update) | async-done | bytes 144
  2419.8 130.7 %reduce-scatter.38.cloned.1.call-done = f32[16,2]{1,0:T(8,128)} async-done(((f32[512,2]{1,0:T(8,128)}), f32[16,2]{1,0:T(8,128)}) %reduce-scatter.38.cloned.1.call-update) | async-done | bytes 144
  2551.8 130.6 %reduce-scatter.40.cloned.1.call-done = f32[16,2]{1,0:T(8,128)} async-done(((f32[512,2]{1,0:T(8,128)}), f32[16,2]{1,0:T(8,128)}) %reduce-scatter.40.cloned.1.call-update) | async-done | bytes 144
  2683.7 130.5 %reduce-scatter.42.cloned.1.call-done = f32[16,2]{1,0:T(8,128)} async-done(((f32[512,2]{1,0:T(8,128)}), f32[16,2]{1,0:T(8,128)}) %reduce-scatter.42.cloned.1.call-update) | async-done | bytes 144
  2815.5 130.6 %reduce-scatter.44.cloned.1.call-done = f32[16,4]{1,0:T(8,128)} async-done(((f32[512,4]{1,0:T(8,128)}), f32[16,4]{1,0:T(8,128)}) %reduce-scatter.44.cloned.1.call-update) | async-done | bytes 272
  2947.5 130.6 %reduce-scatter.46.cloned.1.call-done = f32[16,4]{1,0:T(8,128)} async-done(((f32[512,4]{1,0:T(8,128)}), f32[16,4]{1,0:T(8,128)}) %reduce-scatter.46.cloned.1.call-update) | async-done | bytes 272
  3079.6 136.0 %reduce-scatter.28.cloned.1.call-done = f32[2,16,512]{2,1,0:T(8,128)} async-done(((f32[2,512,512]{2,1,0:T(8,128)}), f32[2,16,512]{2,1,0:T(8,128)}) %reduce-scatter.28.cloned.1.call-update) | async-done | bytes 65552 | tf_op jit(solution)/shard_map/reduce_scatter | solution.py:447
  3215.6 138.7 %reduce-scatter.30.cloned.1.call-done = f32[2,16,512]{2,1,0:T(8,128)} async-done(((f32[2,512,512]{2,1,0:T(8,128)}), f32[2,16,512]{2,1,0:T(8,128)}) %reduce-scatter.30.cloned.1.call-update) | async-done | bytes 65552 | tf_op jit(solution)/shard_map/reduce_scatter | solution.py:451
  3354.3 139.1 %reduce-scatter.32.cloned.1.call-done = f32[2,16,512]{2,1,0:T(8,128)} async-done(((f32[2,512,512]{2,1,0:T(8,128)}), f32[2,16,512]{2,1,0:T(8,128)}) %reduce-scatter.32.cloned.1.call-update) | async-done | bytes 65552 | tf_op jit(solution)/shard_map/reduce_scatter | solution.py:452
  3493.4 118.6 %reduce-scatter.26.cloned.1.call-done = f32[2,16,1536]{2,1,0:T(8,128)} async-done(((f32[2,512,1536]{2,1,0:T(8,128)}), f32[2,16,1536]{2,1,0:T(8,128)}) %reduce-scatter.26.cloned.1.call-update) | async-done | bytes 196624 | tf_op jit(solution)/shard_map/reduce_scatter | solution.py:446
  (1176 shorter events, 1692.6 us)
Async XLA Ops:
  7.2 2279.2 %reduce-scatter.34.cloned.1.call-start = ((), (), s32[]{:S(2)}) async-start(), calls=%async_computation.15 | async-start | bytes 270336
  149.2 36.2 collective-permute-start.1
  321.9 35.6 collective-permute-start.1
  386.4 49.3 %collective-permute-start.1 = (bf16[1536,512]{0,1:T(8,128)(2,1)}, bf16[1536,512]{0,1:T(8,128)(2,1)}, u32[]{:S(2)}, u32[]{:S(2)}) collective-permute-start(bf16[1536,512]{0,1:T(8,128)(2,1)} %get-tuple-element.3944), channel_id=1, source_target_pairs={{0,1},{1,2},{2,3},{4,5},{5,6},{6,7},{8,9},{9,10},{10,11},{12,13},{... | collective-permute-start | bytes 4718600 | tf_op jit(solution)/shard_map/while/body/eval_jaxpr/ppermute | solution.py:25
  464.4 34.1 collective-permute-start.1
  527.4 137.6 %collective-permute-start.1 = (bf16[1536,512]{0,1:T(8,128)(2,1)}, bf16[1536,512]{0,1:T(8,128)(2,1)}, u32[]{:S(2)}, u32[]{:S(2)}) collective-permute-start(bf16[1536,512]{0,1:T(8,128)(2,1)} %get-tuple-element.3944), channel_id=1, source_target_pairs={{0,1},{1,2},{2,3},{4,5},{5,6},{6,7},{8,9},{9,10},{10,11},{12,13},{... | collective-permute-start | bytes 4718600 | tf_op jit(solution)/shard_map/while/body/eval_jaxpr/ppermute | solution.py:25
  715.2 36.2 %collective-permute-start = (bf16[1536,512]{0,1:T(8,128)(2,1)}, bf16[1536,512]{0,1:T(8,128)(2,1)}, u32[]{:S(2)}, u32[]{:S(2)}) collective-permute-start(bf16[1536,512]{0,1:T(8,128)(2,1)} %get-tuple-element.3480), channel_id=1, source_target_pairs={{1,0},{2,1},{3,2},{5,4},{6,5},{7,6},{9,8},{10,9},{11,10},{13,12},{... | collective-permute-start | bytes 4718600 | tf_op jit(solution)/shard_map/while/body/eval_jaxpr/ppermute | solution.py:25
  795.3 46.8 %collective-permute-start = (bf16[1536,512]{0,1:T(8,128)(2,1)}, bf16[1536,512]{0,1:T(8,128)(2,1)}, u32[]{:S(2)}, u32[]{:S(2)}) collective-permute-start(bf16[1536,512]{0,1:T(8,128)(2,1)} %get-tuple-element.3480), channel_id=1, source_target_pairs={{1,0},{2,1},{3,2},{5,4},{6,5},{7,6},{9,8},{10,9},{11,10},{13,12},{... | collective-permute-start | bytes 4718600 | tf_op jit(solution)/shard_map/while/body/eval_jaxpr/ppermute | solution.py:25
  886.2 426.0 %collective-permute-start = (bf16[1536,512]{0,1:T(8,128)(2,1)}, bf16[1536,512]{0,1:T(8,128)(2,1)}, u32[]{:S(2)}, u32[]{:S(2)}) collective-permute-start(bf16[1536,512]{0,1:T(8,128)(2,1)} %get-tuple-element.3480), channel_id=1, source_target_pairs={{1,0},{2,1},{3,2},{5,4},{6,5},{7,6},{9,8},{10,9},{11,10},{13,12},{... | collective-permute-start | bytes 4718600 | tf_op jit(solution)/shard_map/while/body/eval_jaxpr/ppermute | solution.py:25
  911.8 400.4 %copy-start.90 = (f32[2,512]{1,0:T(2,128)S(1)}, f32[2,512]{1,0:T(2,128)}, u32[]{:S(2)}) copy-start(f32[2,512]{1,0:T(2,128)} %copy-done.89) | copy-start | bytes 12292 | tf_op jit(solution)/shard_map/while
  911.8 400.4 %copy-start.94 = (f32[2,512]{1,0:T(2,128)S(1)}, f32[2,512]{1,0:T(2,128)}, u32[]{:S(2)}) copy-start(f32[2,512]{1,0:T(2,128)} %copy-done.93) | copy-start | bytes 12292 | tf_op jit(solution)/shard_map/while
  911.8 400.4 %copy-start.98 = (f32[2,512]{1,0:T(2,128)S(1)}, f32[2,512]{1,0:T(2,128)}, u32[]{:S(2)}) copy-start(f32[2,512]{1,0:T(2,128)} %copy-done.97) | copy-start | bytes 12292 | tf_op jit(solution)/shard_map/while
  1699.0 33.7 collective-permute-start
  2119.7 32.8 collective-permute-start
  2156.7 261.7 %reduce-scatter.36.cloned.1.call-start = ((), (), s32[]{:S(2)}) async-start(), calls=%async_computation.16 | async-start | bytes 270336
  2158.3 392.1 %reduce-scatter.38.cloned.1.call-start = ((), (), s32[]{:S(2)}) async-start(), calls=%async_computation.17 | async-start | bytes 270336
  2159.9 522.4 %reduce-scatter.40.cloned.1.call-start = ((), (), s32[]{:S(2)}) async-start(), calls=%async_computation.18 | async-start | bytes 270336
  2161.7 652.5 %reduce-scatter.42.cloned.1.call-start = ((), (), s32[]{:S(2)}) async-start(), calls=%async_computation.19 | async-start | bytes 270336
  2163.3 782.8 %reduce-scatter.44.cloned.1.call-start = ((), (), s32[]{:S(2)}) async-start(), calls=%async_computation.20 | async-start | bytes 270336
  2165.3 912.8 %reduce-scatter.46.cloned.1.call-start = ((), (), s32[]{:S(2)}) async-start(), calls=%async_computation.21 | async-start | bytes 270336
  2166.7 1048.8 %reduce-scatter.28.cloned.1.call-start = ((), (), s32[]{:S(2)}) async-start(), calls=%async_computation.12 | async-start | bytes 2162688 | tf_op jit(solution)/shard_map/reduce_scatter | solution.py:447
  2167.5 1186.8 %reduce-scatter.30.cloned.1.call-start = ((), (), s32[]{:S(2)}) async-start(), calls=%async_computation.13 | async-start | bytes 2162688 | tf_op jit(solution)/shard_map/reduce_scatter | solution.py:451
  2169.4 1324.0 %reduce-scatter.32.cloned.1.call-start = ((), (), s32[]{:S(2)}) async-start(), calls=%async_computation.14 | async-start | bytes 2162688 | tf_op jit(solution)/shard_map/reduce_scatter | solution.py:452
  2170.0 1442.0 %reduce-scatter.26.cloned.1.call-start = ((), (), s32[]{:S(2)}) async-start(), calls=%async_computation.11 | async-start | bytes 6488064 | tf_op jit(solution)/shard_map/reduce_scatter | solution.py:446
  (307 other events, 2412.0 us)
Sparse Core Ops, SparseCore 0:
  2156.9 129.4 reduce-scatter.33
  2288.7 129.7 reduce-scatter.35
  2420.7 129.7 reduce-scatter.37
  2552.6 129.7 reduce-scatter.39
  2684.5 129.7 reduce-scatter.41
  2816.4 129.6 reduce-scatter.43
  2948.3 129.7 reduce-scatter.45
  3081.0 134.4 reduce-scatter.27
  3218.4 135.8 reduce-scatter.29
  3357.1 136.2 reduce-scatter.31
  3499.6 112.3 reduce-scatter.25
where the time goes:
time: 3620 us
  waiting for transfers between devices  2010 us (56%)
  other arithmetic  474 us (13%)
  matrix products  466 us (13%)
  local copies, waits for them, and re-layouts  294 us (8%)
  loops' own time  225 us (6%)
  starting transfers between devices  138 us (4%)
    unnamed x18, waiting for transfers between devices  901 us
    ppermute x10, waiting for transfers between devices, shifted(): return lax.ppermute(block, axis, route)  573 us
    sub x12, other arithmetic, block_probs(): exp_scores = jnp.exp(masked - jnp.max(masked, axis=-1, keepdims=True))  258 us
    reduce_scatter x1, waiting for transfers between devices, per_device(): lax.psum_scatter(total_down, ('dp', 'section'), scatter_dimension=1, tile...  139 us
    reduce_scatter x1, waiting for transfers between devices, per_device(): lax.psum_scatter(total_up, ('dp', 'section'), scatter_dimension=1, tiled=...  139 us
    ppermute x10, starting transfers between devices, shifted(): return lax.ppermute(block, axis, route)  138 us
    reduce_scatter x1, waiting for transfers between devices, per_device(): lax.psum_scatter(total_mix, ('dp', 'section'), scatter_dimension=1, tiled...  136 us
    another operation x5, loops' own time, backward_tick(): lax.switch(jnp.where(is_valid, section_num, section_count), backward_list...  123 us
  transfers between devices with their start and end apart: 21, of which 21 were waited for; matrix products, arithmetic and copies ran while one was open for 5% of the time, Pallas kernels for 0%

commit v1 on v0

v1 whole, which is shorter than its diff:
```python
import jax
import jax.numpy as jnp
from jax import lax
from jax.experimental import pallas as pl
from jax.experimental.pallas import tpu as pltpu
from jax.sharding import PartitionSpec as P

D = 512
HEADS = 8
HEAD_DIM = 64
LONG = 1024
SHORT = 512
EPS = 1e-05
FILL = -1e30
SCALE = HEAD_DIM ** (-0.5)
LOG2E = 1.4426950408889634
SOFT = SCALE * LOG2E
BF = jnp.bfloat16
F32 = jnp.float32
VAUG = HEAD_DIM + 16


def nn(a, b):
    return lax.dot_general(a, b, (((1,), (0,)), ((), ())), preferred_element_type=F32)


def nt(a, b):
    return lax.dot_general(a, b, (((1,), (1,)), ((), ())), preferred_element_type=F32)


def tn(a, b):
    return lax.dot_general(a, b, (((0,), (0,)), ((), ())), preferred_element_type=F32)


def key_counts(length):
    return (length // 2 + length // 8, length)


def by_count(known_count, length, run):
    low = 0
    for size in key_counts(length):
        if low == 0:
            inside = known_count <= size
        elif size == length:
            inside = known_count > low
        else:
            inside = (known_count > low) & (known_count <= size)
        pl.when(inside)(lambda size=size: run(size))
        low = size


def norm_rows(residual):
    center = residual - jnp.mean(residual, axis=-1, keepdims=True)
    inv_std = lax.rsqrt(jnp.mean(center * center, axis=-1, keepdims=True) + EPS)
    return center * inv_std, inv_std


def one_hot_rows(rank_row, size, length):
    return (lax.broadcasted_iota(jnp.int32, (size, length), 0) == rank_row).astype(F32).astype(BF)


def one_hot_cols(rank_col, size):
    length = rank_col.shape[0]
    return (lax.broadcasted_iota(jnp.int32, (length, size), 1) == rank_col).astype(F32).astype(BF)


def put_masked(dst, src, tokens):
    zeros = jnp.zeros((HEAD_DIM, tokens), BF)
    for head in range(HEADS):
        part = (head % 2) * HEAD_DIM
        dst[head, part : part + HEAD_DIM, :] = src[head * HEAD_DIM : (head + 1) * HEAD_DIM, :]
        dst[head, HEAD_DIM - part : 2 * HEAD_DIM - part, :] = zeros


def head_sums(a, b):
    out = []
    for head in range(HEADS):
        rows = slice(head * HEAD_DIM, (head + 1) * HEAD_DIM)
        out.append(jnp.sum(a[rows, :].astype(F32) * b[rows, :].astype(F32), axis=0, keepdims=True))
    return out


def forward_kernel(
    scal, rank_row, unk, u_own, u_oth, w_t, bcol, w_mix, vecs, ff_in, ff_out,
    s_even, s_odd, q_t, ko_t, vo_t, u_c, k_c, mix_t, lse, nrm0, inv0, gp, hid, nrm1, inv1,
    qm, vaug, kb, sd,
):
    half = u_own.shape[0]
    length = 2 * half
    count = scal[1]
    uo = u_own[...]
    own_t = nt(w_t[...], uo)
    q_t[...] = (own_t[:D] + bcol[:, 0:1]).astype(BF)
    ko_t[...] = own_t[D : 2 * D].astype(BF)
    vo_t[...] = (own_t[2 * D :] + bcol[:, 1:2]).astype(BF)
    put_masked(qm, q_t, half)
    for head, row in enumerate(head_sums(q_t, ko_t)):
        sd[head] = row + unk[...]
    ones_rows = (lax.broadcasted_iota(jnp.int32, (16, length), 0) == 0).astype(F32).astype(BF)
    for head in range(HEADS):
        vaug[head * VAUG + HEAD_DIM : (head + 1) * VAUG, :] = ones_rows
    block = min(half, 256)

    def run(size):
        pick = one_hot_rows(rank_row[...], size, length)
        uc = (nn(pick[:, :half], uo) + nn(pick[:, half:], u_oth[...])).astype(BF)
        u_c[:size, :] = uc
        k_c[:size, :] = nt(uc, w_t[D : 2 * D, :]).astype(BF)
        vct = (nt(w_t[2 * D :, :], uc) + bcol[:, 1:2]).astype(BF)
        for head in range(HEADS):
            vaug[head * VAUG : head * VAUG + HEAD_DIM, :size] = vct[head * HEAD_DIM : (head + 1) * HEAD_DIM, :]
        kb[:size, :] = jnp.where(lax.broadcasted_iota(jnp.int32, (size, 128), 0) < count, 0.0, FILL)

        def pair(p, carry):
            kcp = k_c[:size, pl.ds(pl.multiple_of(p * 128, 128), 128)]
            for e in range(2):
                head = 2 * p + e
                vrows = vaug[pl.ds(pl.multiple_of(head * VAUG, 16), VAUG), :size]
                for start in range(0, half, block):
                    cols = slice(start, start + block)
                    scores = nn(kcp, qm[head, :, cols])
                    sdr = sd[head, :, cols]
                    tops, probs = [], []
                    for t in range(0, block, 128):
                        part = scores[:, t : t + 128] + kb[:size, :]
                        top = jnp.maximum(jnp.max(part, axis=0, keepdims=True), sdr[:, t : t + 128])
                        tops.append(top)
                        probs.append(jnp.exp2((part - top) * SOFT).astype(BF))
                    top = jnp.concatenate(tops, axis=1)
                    mixed = nn(vrows, jnp.concatenate(probs, axis=1))
                    pd = jnp.exp2((sdr - top) * SOFT)
                    total = mixed[HEAD_DIM : HEAD_DIM + 1] + pd
                    rows = pl.ds(pl.multiple_of(head * HEAD_DIM, HEAD_DIM), HEAD_DIM)
                    own = vo_t[rows, cols].astype(F32)
                    mix_t[rows, cols] = ((mixed[:HEAD_DIM] + pd * own) / total).astype(BF)
                    lse[head, :, cols] = top * SOFT + jnp.log2(total)
            return carry

        lax.fori_loop(0, HEADS // 2, pair, 0)

    by_count(count, length, run)

    def tail(i, carry):
        rows = pl.ds(pl.multiple_of(i * 128, 128), 128)
        res = u_own[rows, :].astype(F32) + tn(mix_t[:, rows], w_mix[...]) + vecs[0:1, :]
        normed, inv = norm_rows(res)
        nrm0[rows, :] = normed.astype(BF)
        inv0[rows, :] = inv
        even = (normed * vecs[1:2, :] + vecs[2:3, :]).astype(BF)
        s_even[rows, :] = even
        pre = nn(even, ff_in[...]) + vecs[3:4, :]
        cdf = 0.5 + 0.5 * lax.erf(pre * 0.7071067811865476)
        hidden = (pre * cdf).astype(BF)
        hid[rows, :] = hidden
        gp[rows, :] = (cdf + pre * (0.3989422804014327 * jnp.exp(-0.5 * pre * pre))).astype(BF)
        res = even.astype(F32) + nn(hidden, ff_out[...]) + vecs[4:5, :]
        normed, inv = norm_rows(res)
        nrm1[rows, :] = normed.astype(BF)
        inv1[rows, :] = inv
        s_odd[rows, :] = (normed * vecs[5:6, :] + vecs[6:7, :]).astype(BF)
        return carry

    lax.fori_loop(0, half // 128, tail, 0)


def norm_back(grad, normed, inv, gain):
    e = grad * gain
    return inv * (
        e - jnp.mean(e, axis=-1, keepdims=True) - normed * jnp.mean(e * normed, axis=-1, keepdims=True)
    )


def backward_kernel(
    scal, rank_col, unk, g_own, g_oth, s_even, u_own, q_t, ko_t, vo_t, u_c, k_c, mix_t, lse, nrm0, inv0,
    gp, hid, nrm1, inv1, w_t, bvrow, w_mix, vecs, ff_in, ff_out,
    g_in, g_odd, dx_own, dx_oth, d_qkv, d_mix, d_in, d_out, d_vec, d_col,
    db, dpre, dr, qm, dmm, dm_t, delta, kc_t, vc, kb, dq_t, dk_c, dxs,
):
    half = u_own.shape[0]
    length = 2 * half
    count = scal[1]
    d_vec[...] = jnp.zeros_like(d_vec)

    def add_row(slot, value):
        d_vec[slot : slot + 1, :] += jnp.sum(value, axis=0, keepdims=True)

    def head_part(i, carry):
        rows = pl.ds(pl.multiple_of(i * 128, 128), 128)
        grad = g_own[rows, :].astype(F32)
        if g_oth is not None:
            grad = grad + g_oth[rows, :].astype(F32)
            low = grad.astype(BF)
            g_in[rows, :] = low
            grad = low.astype(F32)
        normed = nrm1[rows, :].astype(F32)
        add_row(5, grad * normed)
        add_row(6, grad)
        dres = norm_back(grad, normed, inv1[rows, :], vecs[5:6, :])
        add_row(4, dres)
        low = dres.astype(BF)
        db[rows, :] = low
        dp = nt(low, ff_out[...]) * gp[rows, :].astype(F32)
        add_row(3, dp)
        low = dp.astype(BF)
        dpre[rows, :] = low
        low = (dres + nt(low, ff_in[...])).astype(BF)
        g_odd[rows, :] = low
        grad = low.astype(F32)
        normed = nrm0[rows, :].astype(F32)
        add_row(1, grad * normed)
        add_row(2, grad)
        dres = norm_back(grad, normed, inv0[rows, :], vecs[1:2, :])
        add_row(0, dres)
        dr[rows, :] = dres
        return carry

    lax.fori_loop(0, half // 128, head_part, 0)
    d_out[...] = tn(hid[...], db[...])
    d_in[...] = tn(s_even[...], dpre[...])
    db[...] = dr[...].astype(BF)
    d_mix[...] = nn(mix_t[...], db[...])
    dmt = nt(w_mix[...], db[...])
    dm_t[...] = dmt.astype(BF)
    d_col[:, 1:2] = jnp.sum(dm_t[...].astype(F32), axis=1, keepdims=True)
    put_masked(qm, q_t, half)
    put_masked(dmm, dm_t, half)
    for head, row in enumerate(head_sums(dm_t, mix_t)):
        delta[head] = row
    block = min(half, 256)

    def run(size):
        uc = u_c[:size, :]
        kc_t[:, :size] = nt(w_t[D : 2 * D, :], uc).astype(BF)
        vc[:size, :] = (nt(uc, w_t[2 * D :, :]) + bvrow[...]).astype(BF)
        kb[:size, :] = jnp.where(lax.broadcasted_iota(jnp.int32, (size, 128), 0) < count, 0.0, FILL)

        def pair(p, carry):
            lanes = pl.ds(pl.multiple_of(p * 128, 128), 128)
            kcp = k_c[:size, lanes]
            vcp = vc[:size, lanes]
            dk = jnp.zeros((size, 128), F32)
            dv = jnp.zeros((size, 128), F32)
            for e in range(2):
                head = 2 * p + e
                rows = pl.ds(pl.multiple_of(head * HEAD_DIM, HEAD_DIM), HEAD_DIM)
                for start in range(0, half, block):
                    cols = slice(start, start + block)
                    qtm = qm[head, :, cols]
                    dmh = dmm[head, :, cols]
                    scores = nn(kcp, qtm)
                    dprob = nn(vcp, dmh)
                    lser = lse[head, :, cols]
                    delr = delta[head, :, cols]
                    lows, grads = [], []
                    for t in range(0, block, 128):
                        tile = slice(t, t + 128)
                        prob = jnp.exp2(jnp.minimum(scores[:, tile] * SOFT - lser[:, tile], kb[:size, :]))
                        lows.append(prob.astype(BF))
                        grads.append((prob * (dprob[:, tile] - delr[:, tile])).astype(BF))
                    low = jnp.concatenate(lows, axis=1)
                    ds = jnp.concatenate(grads, axis=1)
                    dv = dv + nt(low, dmh)
                    dk = dk + nt(ds, qtm)
                    dq_t[rows, cols] = nn(kc_t[rows, :size], ds) * SCALE
            dk_c[:size, lanes] = (dk * SCALE).astype(BF)
            dk_c[:size, pl.ds(pl.multiple_of(D + p * 128, 128), 128)] = dv.astype(BF)
            return carry

        lax.fori_loop(0, HEADS // 2, pair, 0)
        dkv = dk_c[:size, :]
        d_qkv[:, D:] = tn(uc, dkv)
        dxc = nn(dkv, w_t[D:, :]).astype(BF)
        dxs[...] = nn(one_hot_cols(rank_col[:half, :], size), dxc)
        dx_oth[...] = nn(one_hot_cols(rank_col[half:, :], size), dxc).astype(BF)

    by_count(count, length, run)

    dp_t = dmm_rows = None
    sds = head_sums(q_t, ko_t)
    dps = head_sums(dm_t, vo_t)
    dk_parts, dv_parts, dq_parts = [], [], []
    for head in range(HEADS):
        rows = slice(head * HEAD_DIM, (head + 1) * HEAD_DIM)
        prob = jnp.exp2(jnp.minimum(sds[head] * SOFT - lse[head], unk[...]))
        ds = (prob * (dps[head] - delta[head])).astype(BF).astype(F32) * SCALE
        low = prob.astype(BF).astype(F32)
        dq_parts.append(dq_t[rows, :] + ds * ko_t[rows, :].astype(F32))
        dk_parts.append((ds * q_t[rows, :].astype(F32)).astype(BF))
        dv_parts.append((low * dm_t[rows, :].astype(F32)).astype(BF))
    dq = jnp.concatenate(dq_parts, axis=0)
    d_col[:, 0:1] = jnp.sum(dq, axis=1, keepdims=True)
    dp_t = jnp.concatenate([dq.astype(BF)] + dk_parts + dv_parts, axis=0)
    u_t = u_own[...].T
    dw = nt(u_t, dp_t)
    d_qkv[:, :D] = dw[:, :D]
    d_qkv[:, D:] += dw[:, D:]
    dx_own[...] = dr[...] + dxs[...] + tn(dp_t, w_t[...])


def full(shape):
    zeros = (0,) * len(shape)
    return pl.BlockSpec(shape, lambda i, s: zeros)


def shape_of(shape, dtype=BF):
    return jax.ShapeDtypeStruct(shape, dtype)


VMEM_LIMIT = 56 * 1024 * 1024


def call(kernel, scal, ins, in_specs, outs, scratch, flops):
    return pl.pallas_call(
        kernel,
        grid_spec=pltpu.PrefetchScalarGridSpec(
            num_scalar_prefetch=1,
            grid=(1,),
            in_specs=in_specs,
            out_specs=[full(o.shape) for o in outs],
            scratch_shapes=scratch,
        ),
        out_shape=outs,
        compiler_params=pltpu.CompilerParams(vmem_limit_bytes=VMEM_LIMIT),
        cost_estimate=pl.CostEstimate(flops=flops, bytes_accessed=12 * 2**20, transcendentals=2**20),
    )(scal, *ins)


def forward_layer(scal, rank_row, unk, u_own, u_oth, weights, half, own_spec=None, oth_spec=None):
    length = 2 * half
    w_t, bcol, bvrow, w_mix, vecs, ff_in, ff_out = weights
    ins = [rank_row, unk, u_own, u_oth, w_t, bcol, w_mix, vecs, ff_in, ff_out]
    specs = [full(x.shape) for x in ins]
    if own_spec is not None:
        specs[2], specs[3] = own_spec, oth_spec
    tok = shape_of((half, D))
    feat = shape_of((D, half))
    col = shape_of((half, 1), F32)
    outs = [
        tok, tok, feat, feat, feat, shape_of((length, D)), shape_of((length, D)), feat,
        shape_of((HEADS, 1, half), F32), tok, col, tok, tok, tok, col,
    ]
    scratch = [
        pltpu.VMEM((HEADS, 128, half), BF),
        pltpu.VMEM((HEADS * VAUG, length), BF),
        pltpu.VMEM((length, 128), F32),
        pltpu.VMEM((HEADS, 1, half), F32),
    ]
    return call(forward_kernel, scal, ins, specs, outs, scratch, half * 2**23)


def backward_layer(scal, rank_col, unk, g_own, g_oth, u_own, saved, weights, half, u_spec=None):
    length = 2 * half
    w_t, bcol, bvrow, w_mix, vecs, ff_in, ff_out = weights
    s_even, s_odd, q_t, ko_t, vo_t, u_c, k_c, mix_t, lse, nrm0, inv0, gp, hid, nrm1, inv1 = saved
    ins = [
        rank_col, unk, g_own, g_oth, s_even, u_own, q_t, ko_t, vo_t, u_c, k_c, mix_t, lse, nrm0, inv0,
        gp, hid, nrm1, inv1, w_t, bvrow, w_mix, vecs, ff_in, ff_out,
    ]
    tok = shape_of((half, D))
    square = shape_of((D, D), F32)
    outs = [tok, tok, shape_of((half, D), F32), tok, shape_of((D, 3 * D), F32), square, square, square,
            shape_of((8, D), F32), shape_of((D, 2), F32)]
    specs = [None if x is None else full(x.shape) for x in ins]
    if u_spec is not None:
        specs[5] = u_spec
    kernel = backward_kernel
    if g_oth is None:
        del ins[3], specs[3], outs[0]

        def kernel(scal, rank_col, unk, g_own, *rest):
            saved_refs, out_refs = rest[:21], rest[21:]
            backward_kernel(scal, rank_col, unk, g_own, None, *saved_refs, None, *out_refs)

    scratch = [
        pltpu.VMEM((half, D), BF),
        pltpu.VMEM((half, D), BF),
        pltpu.VMEM((half, D), F32),
        pltpu.VMEM((HEADS, 128, half), BF),
        pltpu.VMEM((HEADS, 128, half), BF),
        pltpu.VMEM((D, half), BF),
        pltpu.VMEM((HEADS, 1, half), F32),
        pltpu.VMEM((D, length), BF),
        pltpu.VMEM((length, D), BF),
        pltpu.VMEM((length, 128), F32),
        pltpu.VMEM((D, half), F32),
        pltpu.VMEM((length, 2 * D), BF),
        pltpu.VMEM((half, D), F32),
    ]
    out = call(kernel, scal, ins, specs, outs, scratch, half * 2**24)
    return ([None] + list(out)) if g_oth is None else out


def make_per_device(dp_count, section_count):
    both = ("dp", "section")

    def index(dp, section):
        return dp * section_count + section

    mate_pairs = [
        (index(d, s), index(d ^ 1, s)) for d in range(dp_count) for s in range(section_count)
    ]
    fetch_pairs = [
        (index(d, s), index(d ^ 1, s))
        for d in range(dp_count)
        for s in range(section_count)
        if d % 2 == s // 2
    ]

    def per_device(
        block_input, known_genes, attn_proj, attn_out, query_bias, value_bias, out_bias, ff_in, ff_out,
        ff_bias_in, ff_bias_out, norm_gain, norm_shift, cotangent,
    ):
        core = lax.axis_index("dp") % 2
        section = lax.axis_index("section")
        owner = section // 2
        slot = section % 2

        def row_of(array):
            local = lax.dynamic_index_in_dim(array, slot, 0, keepdims=False)
            sent = lax.ppermute(local, both, fetch_pairs)
            return jnp.where(core == owner, local, sent)

        known = row_of(known_genes)
        row = row_of(block_input)
        cot = row_of(cotangent)

        layers = []
        w_t_all = jnp.swapaxes(attn_proj, 1, 2)
        bcols = jnp.stack([query_bias, value_bias], axis=2)
        zero = jnp.zeros((2, D), F32)
        vecs_all = jnp.stack(
            [out_bias, norm_gain[:, 0], norm_shift[:, 0], ff_bias_in, ff_bias_out, norm_gain[:, 1], norm_shift[:, 1], zero],
            axis=1,
        )
        for layer in range(2):
            layers.append(
                (w_t_all[layer], bcols[layer], value_bias[layer][None], attn_out[layer], vecs_all[layer], ff_in[layer], ff_out[layer])
            )

        cells = []
        for start, length in ((0, LONG), (LONG, SHORT)):
            half = length // 2
            parts = known[start : start + length].reshape(2, half)
            own = lax.dynamic_index_in_dim(parts, core, 0, keepdims=False)
            oth = lax.dynamic_index_in_dim(parts, 1 - core, 0, keepdims=False)
            order = jnp.concatenate([own, oth])
            ids = lax.iota(jnp.int32, length)
            rank = jnp.sum(jnp.where(ids[None, :] <= ids[:, None], order[None, :], 0), axis=1) - 1
            rank = jnp.where(order == 1, rank, -1)
            unk = jnp.where(own == 1, FILL, 0.0).astype(F32)[None]
            scal = jnp.stack([core, jnp.sum(order)]).astype(jnp.int32)
            base = start // half
            blocks = row.reshape(-1, half, D)
            own_spec = pl.BlockSpec((None, half, D), lambda i, s, base=base: (base + s[0], 0, 0))
            oth_spec = pl.BlockSpec((None, half, D), lambda i, s, base=base: (base + 1 - s[0], 0, 0))
            cells.append(dict(half=half, scal=scal, row=rank[None], col=rank[:, None], unk=unk, blocks=blocks,
                              own=own_spec, oth=oth_spec, start=start))

        def mate(x):
            return lax.ppermute(x, both, mate_pairs)

        for cell in cells:
            cell["f0"] = forward_layer(cell["scal"], cell["row"], cell["unk"], cell["blocks"], cell["blocks"], layers[0],
                                       cell["half"], cell["own"], cell["oth"])
            cell["x1"] = cell["f0"][1]
            cell["x1o"] = mate(cell["x1"])
        for cell in cells:
            cell["f1"] = forward_layer(cell["scal"], cell["row"], cell["unk"], cell["x1"], cell["x1o"], layers[1], cell["half"])
        for cell in cells:
            half = cell["half"]
            cots = lax.dynamic_index_in_dim(
                cot[cell["start"] : cell["start"] + 2 * half].reshape(2, half, D), core, 0, keepdims=False
            )
            cell["b1"] = backward_layer(cell["scal"], cell["col"], cell["unk"], cots, None, cell["x1"], cell["f1"], layers[1], half)
            cell["b1o"] = mate(cell["b1"][3])
        for cell in cells:
            half = cell["half"]
            cell["b0"] = backward_layer(cell["scal"], cell["col"], cell["unk"], cell["b1"][2], cell["b1o"], cell["blocks"], cell["f0"],
                                        layers[0], half, cell["own"])
            cell["b0o"] = mate(cell["b0"][3])
            cell["g0"] = (cell["b0"][2] + cell["b0o"].astype(F32)).astype(BF)

        def place(parts):
            got = lax.all_to_all(parts, "section", 0, 0)
            mine = lax.dynamic_slice_in_dim(got, 2 * core, 2, 0)
            theirs = mate(lax.dynamic_slice_in_dim(got, 2 - 2 * core, 2, 0))
            first = jnp.where(core == 0, mine, theirs)
            second = jnp.where(core == 0, theirs, mine)
            lh, sh = LONG // 2, SHORT // 2
            return jnp.concatenate([first[:, :lh], second[:, :lh], first[:, lh:], second[:, lh:]], axis=1)[None]

        outs = jnp.stack([
            jnp.concatenate([cells[0][f][k], cells[1][f][k]], axis=0) for f, k in (("f0", 0), ("f0", 1), ("f1", 0), ("f1", 1))
        ])
        grads = jnp.stack([
            jnp.concatenate(p, axis=0)
            for p in (
                [c["g0"] for c in cells], [c["b0"][1] for c in cells], [c["b0"][0] for c in cells], [c["b1"][1] for c in cells],
            )
        ])
        section_outputs = place(outs)
        section_grads = place(grads)

        def both_layers(k):
            return jnp.stack([sum(c[b][k] for c in cells) for b in ("b0", "b1")])

        tot_qkv, tot_mix, tot_in, tot_out, tot_vec, tot_col = [both_layers(k) for k in range(4, 10)]
        vec = [tot_vec[:, k] for k in range(7)] + [tot_col[:, :, 0], tot_col[:, :, 1]]
        total = dp_count * section_count

        def blocks(x, width):
            return jnp.moveaxis(x.reshape(2, total, -1), 1, 0).reshape(total, 2 * width)

        size = D // total
        widths = [size * 3 * D] + [size * D] * 3 + [size] * 9
        packed = jnp.concatenate(
            [blocks(x, w) for x, w in zip([tot_qkv, tot_mix, tot_in, tot_out] + vec, widths)], axis=1
        ).astype(BF)
        width = packed.shape[1]
        held = packed.reshape(dp_count, section_count, width)
        me = lax.axis_index("dp")
        bits = dp_count.bit_length() - 1
        kept = held.reshape((2,) * bits + (section_count, width))
        for bit in range(bits):
            axis = bits - 1 - bit
            mine = (me >> bit) & 1
            keep = lax.dynamic_index_in_dim(kept, mine, axis, keepdims=True)
            send = lax.dynamic_index_in_dim(kept, 1 - mine, axis, keepdims=True)
            pairs = [
                (index(d, s), index(d ^ (1 << bit), s)) for d in range(dp_count) for s in range(section_count)
            ]
            kept = (keep.astype(F32) + lax.ppermute(send, both, pairs).astype(F32)).astype(BF)
        kept = kept.reshape(section_count, width)
        final = jnp.sum(lax.all_to_all(kept, "section", 0, 0).astype(F32), axis=0)
        pieces, at = [], 0
        for w in widths:
            pieces.append(final[at : at + 2 * w])
            at += 2 * w
        g_qkv = pieces[0].reshape(2, size, 3 * D)
        g_mix, g_in, g_out = [x.reshape(2, size, D) for x in pieces[1:4]]
        v = [x.reshape(2, size) for x in pieces[4:]]
        return (
            section_outputs, section_grads, g_qkv, g_mix, v[7], v[8], v[0], g_in, g_out, v[3], v[4],
            jnp.stack([v[1], v[5]], axis=1), jnp.stack([v[2], v[6]], axis=1),
        )

    return per_device


def solution(mesh):
    rows = P("dp", None, None)
    placed = (rows, P("dp", None)) + (P(),) * 11 + (rows,)
    sections = P("section", "dp", None, None)
    matrix = P(None, ("dp", "section"), None)
    vector = P(None, ("dp", "section"))
    pairs = P(None, None, ("dp", "section"))
    return jax.shard_map(
        make_per_device(mesh.shape["dp"], mesh.shape["section"]),
        mesh=mesh,
        in_specs=placed,
        out_specs=(
            sections, sections, matrix, matrix, vector, vector, vector, matrix, matrix, vector, vector, pairs, pairs,
        ),
        check_vma=False,
    )
```

time: 3620 us -> 545 us (0.15)
  waiting for transfers between devices: 2010 us -> 137 us
  matrix products: 466 us -> 0 us
  other arithmetic: 474 us -> 91.2 us
  loops' own time: 225 us -> 0 us
  local copies, waits for them, and re-layouts: 294 us -> 134 us
  Pallas kernels: 0 us -> 139 us
  starting transfers between devices: 138 us -> 27.9 us
    unnamed x18 -> x0, waiting for transfers between devices: 901 us -> none
    ppermute x10 -> x14, waiting for transfers between devices: 573 us -> 27.2 us  [the longest x3 27.2 us: per_device(): lax.ppermute(send, both, pairs).astype(F32)]
    reduce_scatter x4 -> x0, waiting for transfers between devices: 532 us -> none  [the longest x1 139 us: per_device(): lax.psum_scatter(total_down, ('dp', 'section'), scatter_dimension=1, tile...]
    dot_general x64 -> x0, matrix products: 444 us -> none  [the longest x12 102 us: block_probs(): jnp.einsum('qhd,khd->hqk', query_block, key_heads, preferred_element_type...]
    sub x12 -> x2, other arithmetic: 258 us -> 0.59 us  [per_device(): jnp.sum(jnp.where(ids[None, :] <= ids[:, None], order[None, :], 0), axis=1)]
    another operation x18 -> x0, loops' own time: 225 us -> none  [the longest x5 123 us: backward_tick(): lax.switch(jnp.where(is_valid, section_num, section_count), backward_list...]
    pallas_call x0 -> x8, Pallas kernels: none -> 139 us  [call(): pl.pallas_call(kernel, grid_spec=pltpu.PrefetchScalarGridSpec(num_scalar_...]
    ppermute x10 -> x14, starting transfers between devices: 138 us -> 14.4 us  [the longest x3 7.31 us: row_of(): sent = lax.ppermute(local, both, fetch_pairs)]
  transfers between devices with their start and end apart: 21 -> 17, of which waited for: 21 -> 5; matrix products, arithmetic and copies ran while one was open for 5% -> 20% of each run, Pallas kernels for 0% -> 21%
where the time goes in v1:
time: 545 us; the launch traced here: 535 us
  Pallas kernels  139 us (26%)
  waiting for transfers between devices  137 us (25%)
  local copies, waits for them, and re-layouts  134 us (25%)
  other arithmetic  91.2 us (17%)
  starting transfers between devices  27.9 us (5%)
    pallas_call x8, Pallas kernels, call(): pl.pallas_call(kernel, grid_spec=pltpu.PrefetchScalarGridSpec(num_scalar_...  139 us
    all_to_all x2, waiting for transfers between devices, place(): got = lax.all_to_all(parts, 'section', 0, 0)  95.8 us
    unnamed x107, local copies, waits for them, and re-layouts  42.7 us
    another operation x10, local copies, waits for them, and re-layouts, both_layers(): return jnp.stack([sum((c[b][k] for c in cells)) for b in ('b0', 'b1')])  32.3 us
    ppermute x3, waiting for transfers between devices, per_device(): lax.ppermute(send, both, pairs).astype(F32)  27.2 us
    transpose x4, other arithmetic, blocks(): return jnp.moveaxis(x.reshape(2, total, -1), 1, 0).reshape(total, 2 * width)  22.3 us
    another operation x10, other arithmetic  18.1 us
    all_to_all x1, waiting for transfers between devices, per_device(): final = jnp.sum(lax.all_to_all(kept, 'section', 0, 0).astype(F32), axis=0)  14.3 us
  transfers between devices with their start and end apart: 17, of which 5 were waited for; matrix products, arithmetic and copies ran while one was open for 20% of the time, Pallas kernels for 21%

profile of v1, /device:TPU:0, one launch (start us, length us, event | category | flops | bytes accessed | tf_op | source)
XLA Modules:
  0.0 534.7 jit_solution(2257172776227285620)
XLA Ops:
  44.4 10.8 %shard_map.238 = (bf16[256,512]{1,0:T(8,128)(2,1)}, bf16[256,512]{1,0:T(8,128)(2,1)}, bf16[512,256]{1,0:T(8,128)(2,1)}, bf16[512,256]{1,0:T(8,128)(2,1)}, bf16[5...) custom-call(s32[2]{0:T(128)} %get-tuple-element.326.scal, ...), custom_call_target="tpu_custom_call" | custom-call | flops 2147483648 | bytes 12582912 | tf_op jit(solution)/shard_map/pallas_call | solution.py:313
  55.5 19.6 %shard_map.237 = (bf16[512,512]{1,0:T(8,128)(2,1)}, bf16[512,512]{1,0:T(8,128)(2,1)}, bf16[512,512]{1,0:T(8,128)(2,1)}, bf16[512,512]{1,0:T(8,128)(2,1)}, bf16[5...) custom-call(s32[2]{0:T(128)} %get-tuple-element.325.scal, ...), custom_call_target="tpu_custom_call" | custom-call | flops 4294967296 | bytes 12582912 | tf_op jit(solution)/shard_map/pallas_call | solution.py:313
  80.3 10.8 %shard_map.240 = (bf16[256,512]{1,0:T(8,128)(2,1)}, bf16[256,512]{1,0:T(8,128)(2,1)}, bf16[512,256]{1,0:T(8,128)(2,1)}, bf16[512,256]{1,0:T(8,128)(2,1)}, bf16[5...) custom-call(s32[2]{0:T(128)} %get-tuple-element.326.scal, ...), custom_call_target="tpu_custom_call" | custom-call | flops 2147483648 | bytes 12582912 | tf_op jit(solution)/shard_map/pallas_call | solution.py:313
  91.2 14.6 %shard_map.243 = (bf16[256,512]{1,0:T(8,128)(2,1)}, f32[256,512]{1,0:T(8,128)}, bf16[256,512]{1,0:T(8,128)(2,1)}, f32[512,1536]{1,0:T(8,128)}, f32[512,512]{1,0:...) custom-call(s32[2]{0:T(128)} %get-tuple-element.326.scal, ...), custom_call_target="tpu_custom_call" | custom-call | flops 4294967296 | bytes 12582912 | tf_op jit(solution)/shard_map/pallas_call | solution.py:313
  106.7 19.8 %shard_map.239 = (bf16[512,512]{1,0:T(8,128)(2,1)}, bf16[512,512]{1,0:T(8,128)(2,1)}, bf16[512,512]{1,0:T(8,128)(2,1)}, bf16[512,512]{1,0:T(8,128)(2,1)}, bf16[5...) custom-call(s32[2]{0:T(128)} %get-tuple-element.325.scal, ...), custom_call_target="tpu_custom_call" | custom-call | flops 4294967296 | bytes 12582912 | tf_op jit(solution)/shard_map/pallas_call | solution.py:313
  126.5 24.4 %shard_map.241 = (bf16[512,512]{1,0:T(8,128)(2,1)}, f32[512,512]{1,0:T(8,128)}, bf16[512,512]{1,0:T(8,128)(2,1)}, f32[512,1536]{1,0:T(8,128)}, f32[512,512]{1,0:...) custom-call(s32[2]{0:T(128)} %get-tuple-element.325.scal, ...), custom_call_target="tpu_custom_call" | custom-call | flops 8589934592 | bytes 12582912 | tf_op jit(solution)/shard_map/pallas_call | solution.py:313
  162.9 7.7 %stack.170 = bf16[1,32,24576]{2,0,1:T(2,128)(2,1)S(1)} reshape(bf16[512,1536]{1,0:T(8,128)(2,1)} %add_convert_fusion.2) | data formatting | bytes 3145728 | tf_op jit(solution)/shard_map/stack | solution.py:505
  170.7 14.9 %shard_map.244 = (bf16[256,512]{1,0:T(8,128)(2,1)}, bf16[256,512]{1,0:T(8,128)(2,1)}, f32[256,512]{1,0:T(8,128)}, bf16[256,512]{1,0:T(8,128)(2,1)}, f32[512,1536...) custom-call(s32[2]{0:T(128)} %get-tuple-element.326.scal, ...), custom_call_target="tpu_custom_call" | custom-call | flops 4294967296 | bytes 12582912 | tf_op jit(solution)/shard_map/pallas_call | solution.py:313
  185.6 24.5 %shard_map.242 = (bf16[512,512]{1,0:T(8,128)(2,1)}, bf16[512,512]{1,0:T(8,128)(2,1)}, f32[512,512]{1,0:T(8,128)}, bf16[512,512]{1,0:T(8,128)(2,1)}, f32[512,1536...) custom-call(s32[2]{0:T(128)} %get-tuple-element.325.scal, ...), custom_call_target="tpu_custom_call" | custom-call | flops 8589934592 | bytes 12582912 | tf_op jit(solution)/shard_map/pallas_call | solution.py:313
  218.5 4.4 maximum_bitcast_fusion.5
  231.3 4.4 maximum_bitcast_fusion.4
  251.0 4.5 add_convert_fusion.3
  255.4 9.0 %stack.169 = bf16[1,32,24576]{2,0,1:T(2,128)(2,1)} reshape(bf16[512,1536]{1,0:T(8,128)(2,1)} %add_convert_fusion.3) | data formatting | bytes 3145728 | tf_op jit(solution)/shard_map/stack | solution.py:505
  264.4 9.1 %maximum_bitcast_fusion.2 = bf16[32,2,24576]{2,1,0:T(2,128)(2,1)} fusion(bf16[1,32,24576]{2,0,1:T(2,128)(2,1)S(1)} %stack.170, bf16[1,32,24576]{2,0,1:T(2,128)(2,1)} %stack.169), kind=kLoop, calls=%fused_computation.8 | loop fusion | flops 6291456 | bytes 6291456 | tf_op jit(solution)/shard_map/transpose | solution.py:512
  273.5 5.4 %concatenate.139 = bf16[2,2,2,4,49152]{4,3,2,1,0:T(4,128)(2,1)S(1)} reshape(bf16[32,2,24576]{2,1,0:T(2,128)(2,1)} %maximum_bitcast_fusion.2) | data formatting | bytes 6291456 | tf_op jit(solution)/shard_map/concatenate | solution.py:516
  310.3 5.8 %collective-permute-done.11 = bf16[2,2,1,4,98592]{4,3,2,1,0:T(4,128)(2,1)} collective-permute-done((bf16[2,2,1,4,98592]{4,3,2,1,0:T(4,128)(2,1)S(1)}, bf16[2,2,1,4,98592]{4,3,2,1,0:T(4,128)(2,1)}, u32[]{:S(2)}, u32[]{:S(2)}) %collective-permute-start.11) | collective-permute-done | bytes 3154976 | tf_op jit(solution)/shard_map/ppermute | solution.py:532
  316.1 4.5 add_convert_fusion
  329.1 5.4 %all-to-all-start = ((bf16[4,768,512]{2,1,0:T(8,128)(2,1)}), bf16[4,768,512]{2,1,0:T(8,128)(2,1)}, u32[]{:S(2)}, u32[]{:S(2)}) async-start(bf16[4,768,512]{2,1,0:T(8,128)(2,1)} %pad_maximum_fusion), calls=%async_computation | async-start | bytes 6291456 | tf_op jit(solution)/shard_map/all_to_all | solution.py:484
  338.4 21.4 %collective-permute-done.12 = bf16[2,1,1,4,98592]{4,3,2,1,0:T(4,128)(2,1)} collective-permute-done((bf16[2,1,1,4,98592]{4,3,2,1,0:T(4,128)(2,1)}, bf16[2,1,1,4,98592]{4,3,2,1,0:T(4,128)(2,1)}, u32[]{:S(2)}, u32[]{:S(2)}) %collective-permute-start.12) | collective-permute-done | bytes 1577504 | tf_op jit(solution)/shard_map/ppermute | solution.py:532
  368.2 37.7 %all-to-all-done = bf16[4,768,512]{2,1,0:T(8,128)(2,1)} async-done(((bf16[4,768,512]{2,1,0:T(8,128)(2,1)}), bf16[4,768,512]{2,1,0:T(8,128)(2,1)}, u32[]{:S(2)}, u32[]{:S(2)}) %all-to-all-start) | async-done | bytes 3145760 | tf_op jit(solution)/shard_map/all_to_all | solution.py:484
  421.9 58.1 %all-to-all-done.1 = bf16[4,768,512]{2,1,0:T(8,128)(2,1)S(1)} async-done(((bf16[4,768,512]{2,1,0:T(8,128)(2,1)}), bf16[4,768,512]{2,1,0:T(8,128)(2,1)S(1)}, u32[]{:S(2)}, u32[]{:S(2)}) %all-to-all-start.1) | async-done | bytes 3145760 | tf_op jit(solution)/shard_map/all_to_all | solution.py:484
  480.0 4.5 all-to-all-start.2
  489.9 14.3 %all-to-all-done.2 = bf16[4,2,49296]{2,1,0:T(2,128)(2,1)} async-done(((bf16[4,2,49296]{2,1,0:T(2,128)(2,1)}), bf16[4,2,49296]{2,1,0:T(2,128)(2,1)}, u32[]{:S(2)}, u32[]{:S(2)}) %all-to-all-start.2) | async-done | bytes 788768 | tf_op jit(solution)/shard_map/all_to_all | solution.py:534
  504.2 4.8 reshape.426
  (291 shorter events, 189.8 us)
Async XLA Ops:
  0.7 11.5 %copy-start.37 = (f32[2,2,512]{2,1,0:T(2,128)S(1)}, f32[2,2,512]{2,1,0:T(2,128)}, u32[]{:S(2)}) copy-start(f32[2,2,512]{2,1,0:T(2,128)} %param.26) | copy-start | bytes 24580
  3.6 39.5 %collective-permute-start.1 = (bf16[1536,512]{1,0:T(8,128)(2,1)}, bf16[1536,512]{1,0:T(8,128)(2,1)}, u32[]{:S(2)}, u32[]{:S(2)}) collective-permute-start(bf16[1536,512]{1,0:T(8,128)(2,1)} %dynamic-slice_bitcast_fusion.1), channel_id=1, source_target_pairs={{0,4},{1,5},{6,2},{7,3},{8,12},{9,13},{14,10},{15,11},{16,20},{17,... | collective-permute-start | bytes 4718600 | tf_op jit(solution)/shard_map/ppermute | solution.py:420
  7.1 17.5 %collective-permute-start = (s32[1536]{0:T(1024)S(1)}, s32[1536]{0:T(1024)S(1)}, u32[]{:S(2)}, u32[]{:S(2)}) collective-permute-start(s32[1536]{0:T(1024)S(1)} %dynamic-slice_reduce_fusion), channel_id=1, source_target_pairs={{0,4},{1,5},{6,2},{7,3},{8,12},{9,13},{14,10},{15,11},{16,20},{17,... | collective-permute-start | bytes 18440 | tf_op jit(solution)/shard_map/ppermute | solution.py:420
  9.7 45.6 %collective-permute-start.5 = (bf16[1536,512]{1,0:T(8,128)(2,1)}, bf16[1536,512]{1,0:T(8,128)(2,1)}, u32[]{:S(2)}, u32[]{:S(2)}) collective-permute-start(bf16[1536,512]{1,0:T(8,128)(2,1)} %dynamic-slice_bitcast_fusion), channel_id=1, source_target_pairs={{0,4},{1,5},{6,2},{7,3},{8,12},{9,13},{14,10},{15,11},{16,20},{17,... | collective-permute-start | bytes 4718600 | tf_op jit(solution)/shard_map/ppermute | solution.py:420
  23.6 19.4 %copy-start.6 = (bf16[2,1536,512]{2,1,0:T(8,128)(2,1)S(1)}, bf16[2,1536,512]{2,1,0:T(8,128)(2,1)}, u32[]{:S(2)}) copy-start(bf16[2,1536,512]{2,1,0:T(8,128)(2,1)} %param.14) | copy-start | bytes 9437188
  55.2 24.4 %collective-permute-start.3 = (bf16[256,512]{1,0:T(8,128)(2,1)}, bf16[256,512]{1,0:T(8,128)(2,1)S(1)}, u32[]{:S(2)}, u32[]{:S(2)}) collective-permute-start(bf16[256,512]{1,0:T(8,128)(2,1)} %get-tuple-element.114.u_own.rest_1_), channel_id=1, source_target_pairs={{0,4},{1,5},{2,6},{3,7},{4,0},{5,1},{6,2},{7,3},{8,12},{9,13},{10,... | collective-permute-start | bytes 786440 | tf_op jit(solution)/shard_map/ppermute | solution.py:460
  76.2 29.7 %collective-permute-start.2 = (bf16[512,512]{1,0:T(8,128)(2,1)S(1)}, bf16[512,512]{1,0:T(8,128)(2,1)S(1)}, u32[]{:S(2)}, u32[]{:S(2)}) collective-permute-start(bf16[512,512]{1,0:T(8,128)(2,1)S(1)} %copy-done.20), channel_id=1, source_target_pairs={{0,4},{1,5},{2,6},{3,7},{4,0},{5,1},{6,2},{7,3},{8,12},{9,13},{10,... | collective-permute-start | bytes 1572872 | tf_op jit(solution)/shard_map/ppermute | solution.py:460
  105.8 64.9 %collective-permute-start.8 = (bf16[256,512]{1,0:T(8,128)(2,1)}, bf16[256,512]{1,0:T(8,128)(2,1)}, u32[]{:S(2)}, u32[]{:S(2)}) collective-permute-start(bf16[256,512]{1,0:T(8,128)(2,1)} %get-tuple-element.163), channel_id=1, source_target_pairs={{0,4},{1,5},{2,6},{3,7},{4,0},{5,1},{6,2},{7,3},{8,12},{9,13},{10,... | collective-permute-start | bytes 786440 | tf_op jit(solution)/shard_map/ppermute | solution.py:460
  126.5 25.0 %copy-start.17 = (f32[512,512]{1,0:T(8,128)S(1)}, f32[512,512]{1,0:T(8,128)}, u32[]{:S(2)}) copy-start(f32[512,512]{1,0:T(8,128)} %get-tuple-element.200) | copy-start | bytes 3145732
  126.5 26.6 %copy-start.16 = (f32[512,512]{1,0:T(8,128)S(1)}, f32[512,512]{1,0:T(8,128)}, u32[]{:S(2)}) copy-start(f32[512,512]{1,0:T(8,128)} %get-tuple-element.196) | copy-start | bytes 3145732
  150.9 34.6 %collective-permute-start.6 = (bf16[512,512]{1,0:T(8,128)(2,1)}, bf16[512,512]{1,0:T(8,128)(2,1)}, u32[]{:S(2)}, u32[]{:S(2)}) collective-permute-start(bf16[512,512]{1,0:T(8,128)(2,1)} %get-tuple-element.133), channel_id=1, source_target_pairs={{0,4},{1,5},{2,6},{3,7},{4,0},{5,1},{6,2},{7,3},{8,12},{9,13},{10,... | collective-permute-start | bytes 1572872 | tf_op jit(solution)/shard_map/ppermute | solution.py:460
  185.5 24.5 %copy-start.25 = (f32[512,2]{1,0:T(8,128)S(1)}, f32[512,2]{1,0:T(8,128)}, u32[]{:S(2)}) copy-start(f32[512,2]{1,0:T(8,128)} %get-tuple-element.206) | copy-start | bytes 12292
  185.5 25.9 %copy-start.34 = (f32[8,512]{1,0:T(8,128)S(1)}, f32[8,512]{1,0:T(8,128)}, u32[]{:S(2)}) copy-start(f32[8,512]{1,0:T(8,128)} %get-tuple-element.202) | copy-start | bytes 49156
  310.2 5.9 %collective-permute-start.11 = (bf16[2,2,1,4,98592]{4,3,2,1,0:T(4,128)(2,1)S(1)}, bf16[2,2,1,4,98592]{4,3,2,1,0:T(4,128)(2,1)}, u32[]{:S(2)}, u32[]{:S(2)}) collective-permute-start(bf16[2,2,1,4,98592]{4,3,2,1,0:T(4,128)(2,1)S(1)} %constant_dynamic-slice_fusion.2), channel_id=1, source_target_pairs={{0,4},{1,5},{2,6},{3,7},{4,0},{5,1},{6,2},{7,3},{8,12},{9,13},{10,... | collective-permute-start | bytes 9464840 | tf_op jit(solution)/shard_map/ppermute | solution.py:532
  322.3 37.5 %collective-permute-start.12 = (bf16[2,1,1,4,98592]{4,3,2,1,0:T(4,128)(2,1)}, bf16[2,1,1,4,98592]{4,3,2,1,0:T(4,128)(2,1)}, u32[]{:S(2)}, u32[]{:S(2)}) collective-permute-start(bf16[2,1,1,4,98592]{4,3,2,1,0:T(4,128)(2,1)} %constant_dynamic-slice_fusion.1), channel_id=1, source_target_pairs={{0,8},{1,9},{2,10},{3,11},{4,12},{5,13},{6,14},{7,15},{8,0},{9,1},... | collective-permute-start | bytes 4732424 | tf_op jit(solution)/shard_map/ppermute | solution.py:532
  327.0 8.7 %collective-permute-start.9 = (bf16[256,512]{1,0:T(8,128)(2,1)}, bf16[256,512]{1,0:T(8,128)(2,1)}, u32[]{:S(2)}, u32[]{:S(2)}) collective-permute-start(bf16[256,512]{1,0:T(8,128)(2,1)} %get-tuple-element.178), channel_id=1, source_target_pairs={{0,4},{1,5},{2,6},{3,7},{4,0},{5,1},{6,2},{7,3},{8,12},{9,13},{10,... | collective-permute-start | bytes 786440 | tf_op jit(solution)/shard_map/ppermute | solution.py:460
  329.1 76.7 %all-to-all-start = ((bf16[4,768,512]{2,1,0:T(8,128)(2,1)}), bf16[4,768,512]{2,1,0:T(8,128)(2,1)}, u32[]{:S(2)}, u32[]{:S(2)}) async-start(bf16[4,768,512]{2,1,0:T(8,128)(2,1)} %pad_maximum_fusion), calls=%async_computation | async-start | bytes 6291456 | tf_op jit(solution)/shard_map/all_to_all | solution.py:484
  336.9 29.2 %collective-permute-start.7 = (bf16[512,512]{1,0:T(8,128)(2,1)}, bf16[512,512]{1,0:T(8,128)(2,1)S(1)}, u32[]{:S(2)}, u32[]{:S(2)}) collective-permute-start(bf16[512,512]{1,0:T(8,128)(2,1)} %get-tuple-element.148), channel_id=1, source_target_pairs={{0,4},{1,5},{2,6},{3,7},{4,0},{5,1},{6,2},{7,3},{8,12},{9,13},{10,... | collective-permute-start | bytes 1572872 | tf_op jit(solution)/shard_map/ppermute | solution.py:460
  338.3 27.7 %copy-start.14 = (f32[512,512]{1,0:T(8,128)S(1)}, f32[512,512]{1,0:T(8,128)}, u32[]{:S(2)}) copy-start(f32[512,512]{1,0:T(8,128)} %get-tuple-element.147) | copy-start | bytes 3145732
  364.3 48.1 %collective-permute-start.13 = (bf16[1,1,1,4,98592]{4,3,2,1,0:T(4,128)(2,1)}, bf16[1,1,1,4,98592]{4,3,2,1,0:T(4,128)(2,1)}, u32[]{:S(2)}, u32[]{:S(2)}) collective-permute-start(bf16[1,1,1,4,98592]{4,3,2,1,0:T(4,128)(2,1)} %constant_dynamic-slice_fusion), channel_id=1, source_target_pairs={{0,16},{1,17},{2,18},{3,19},{4,20},{5,21},{6,22},{7,23},{8,24},{9,... | collective-permute-start | bytes 2366216 | tf_op jit(solution)/shard_map/ppermute | solution.py:532
  405.9 74.1 %all-to-all-start.1 = ((bf16[4,768,512]{2,1,0:T(8,128)(2,1)}), bf16[4,768,512]{2,1,0:T(8,128)(2,1)S(1)}, u32[]{:S(2)}, u32[]{:S(2)}) async-start(bf16[4,768,512]{2,1,0:T(8,128)(2,1)} %pad_maximum_fusion.1), calls=%async_computation.1 | async-start | bytes 6291456 | tf_op jit(solution)/shard_map/all_to_all | solution.py:484
  412.4 73.4 %collective-permute-start.4 = (bf16[2,768,512]{2,1,0:T(8,128)(2,1)}, bf16[2,768,512]{2,1,0:T(8,128)(2,1)}, u32[]{:S(2)}, u32[]{:S(2)}) collective-permute-start(bf16[2,768,512]{2,1,0:T(8,128)(2,1)} %constant_dynamic-slice_fusion.4), channel_id=1, source_target_pairs={{0,4},{1,5},{2,6},{3,7},{4,0},{5,1},{6,2},{7,3},{8,12},{9,13},{10,... | collective-permute-start | bytes 4718600 | tf_op jit(solution)/shard_map/ppermute | solution.py:460
  480.0 24.2 %all-to-all-start.2 = ((bf16[4,2,49296]{2,1,0:T(2,128)(2,1)}), bf16[4,2,49296]{2,1,0:T(2,128)(2,1)}, u32[]{:S(2)}, u32[]{:S(2)}) async-start(bf16[4,2,49296]{2,1,0:T(2,128)(2,1)} %reshape.425), calls=%async_computation.2 | async-start | bytes 1581056 | tf_op jit(solution)/shard_map/all_to_all | solution.py:534
  485.8 44.6 %collective-permute-start.10 = (bf16[2,768,512]{2,1,0:T(8,128)(2,1)}, bf16[2,768,512]{2,1,0:T(8,128)(2,1)}, u32[]{:S(2)}, u32[]{:S(2)}) collective-permute-start(bf16[2,768,512]{2,1,0:T(8,128)(2,1)} %constant_dynamic-slice_fusion.3), channel_id=1, source_target_pairs={{0,4},{1,5},{2,6},{3,7},{4,0},{5,1},{6,2},{7,3},{8,12},{9,13},{10,... | collective-permute-start | bytes 4718600 | tf_op jit(solution)/shard_map/ppermute | solution.py:460
  (38 other events, 174.3 us)
